TPU v7x, 32 devices: a whole 2x2x4 slice. The times are simulated.
32 devices in a mesh: group: 2 (over x), wide: 8 (over z, y), narrow: 2 (over core).
Axes of the slice: x: 2, y: 2, z: 4, core: 2. Of those that a mesh axis runs over, the one named last changes fastest.
Arguments:
- embeds: bfloat16 [4, 64, 5120], P(None, ('group', 'wide'), 'narrow'), parts along dimension 1, may hold values from -120 to 120
- lengths: int32 [64], P(('group', 'wide')), parts along dimension 0, may hold values from 1 to 384, 6144 in all
- k_cache: bfloat16 [64, 8, 384, 128], P(('group', 'wide'), 'narrow'), parts along dimension 0, may hold values from -175 to 175
- v_cache: bfloat16 [64, 8, 384, 128], P(('group', 'wide'), 'narrow'), parts along dimension 0, may hold values from -4 to 4
- gain_attn: bfloat16 [5120], P('narrow'), may hold values from 0.25 to 1.75
- gain_ffn: bfloat16 [5120], P('narrow'), may hold values from 0.25 to 1.75
- w_query: bfloat16 [5120, 5120], P('narrow', 'wide'), may hold values from -0.078125 to 0.078125
- w_key: bfloat16 [5120, 1024], P('narrow', 'wide'), may hold values from -0.078125 to 0.078125
- w_value: bfloat16 [5120, 1024], P('narrow', 'wide'), may hold values from -0.078125 to 0.078125
- w_out: bfloat16 [5120, 5120], P('narrow', 'wide'), may hold values from -0.078125 to 0.078125
- w_gate: bfloat16 [5120, 14336], P('narrow', 'wide'), may hold values from -0.078125 to 0.078125
- w_up: bfloat16 [5120, 14336], P('narrow', 'wide'), may hold values from -0.078125 to 0.078125
- w_down: bfloat16 [14336, 5120], P('wide', 'narrow'), may hold values from -0.046875 to 0.046875
Outputs:
- hidden_out: float32 [4, 64, 5120], P(None, ('group', 'wide'), 'narrow'), parts along dimension 1
- new_keys: bfloat16 [64, 8, 4, 128], P(('group', 'wide'), 'narrow'), parts along dimension 0
- new_values: bfloat16 [64, 8, 4, 128], P(('group', 'wide'), 'narrow'), parts along dimension 0
There are 2 independent parts, one for each index of `group`. A program takes and returns all parts, laid end to end along the dimension named above; an argument that names none is the same for every part. Nothing has to cross between parts.
Inputs may be any that keep to these rules, and one draw needn't show every extreme that they name: In every part one rollout has all 384 cache positions valid, and the lengths of the 32 rollouts of one part sum to 6144.
All inputs are finite; a program needn't handle non-finite values. No bound on the sum of `lengths` on one device may be relied on, other than what follows from the above.
Results may differ from a plain program's by a relative error of at most 0.0051.
Values may be sent and summed in bfloat16 or wider, within the bound.
A program may use at most 128 MiB of HBM per device.

v0:
```python
import math

import jax
import jax.numpy as jnp
from jax import lax
from jax.sharding import PartitionSpec as P

HQ = 40
KVH = 8
HD = 128
STEPS = 4


rope_base = 1000000.0
norm_eps = 1e-06


def angles_for(positions, head_dim):
    steps_up = jnp.arange(head_dim // 2, dtype=jnp.float32)
    inverse = jnp.exp(steps_up * (-2.0 * math.log(rope_base) / head_dim))
    return positions.astype(jnp.float32)[..., None] * inverse


def rotate(values, angles):
    half_dim = values.shape[-1] // 2
    cosine = jnp.cos(angles)
    sine_part = jnp.sin(angles)
    leading = values[..., :half_dim]
    trailing = values[..., half_dim:]
    return jnp.concatenate(
        [leading * cosine - trailing * sine_part, trailing * cosine + leading * sine_part], axis=-1
    )


def scale_rows(tokens, row_sums, gain_row, full_width):
    factor = lax.rsqrt(row_sums / full_width + norm_eps)
    return (tokens * factor[:, None] * gain_row.astype(jnp.float32)).astype(jnp.bfloat16)


def shards(
    embeds,
    lengths,
    k_cache,
    v_cache,
    gain_attn,
    gain_ffn,
    w_query,
    w_key,
    w_value,
    w_out,
    w_gate,
    w_up,
    w_down,
):
    local_rolls = embeds.shape[1]
    half_width = embeds.shape[2]
    full_width = half_width * lax.axis_size("narrow")
    kv_local = k_cache.shape[1]
    cache_len = k_cache.shape[2]
    group_size = HQ // KVH
    heads_local = kv_local * group_size
    query_cols = w_query.shape[1]
    key_cols = w_key.shape[1]
    ffn_cols = w_gate.shape[1]
    score_scale = 1.0 / math.sqrt(HD)
    cache_live = jnp.arange(cache_len, dtype=jnp.int32)[None, :] < lengths[:, None]
    tokens = embeds.reshape(STEPS * local_rolls, half_width).astype(jnp.float32)
    attn_sums = lax.psum(jnp.sum(tokens * tokens, axis=1), "narrow")
    normed = scale_rows(tokens, attn_sums, gain_attn, full_width)
    rows_all = lax.all_gather(normed, "wide", axis=0, tiled=True)
    partial = jnp.concatenate(
        [
            jnp.dot(rows_all, w_query, preferred_element_type=jnp.float32),
            jnp.dot(rows_all, w_key, preferred_element_type=jnp.float32),
            jnp.dot(rows_all, w_value, preferred_element_type=jnp.float32),
        ],
        axis=1,
    )
    full = lax.all_to_all(partial, "wide", split_axis=0, concat_axis=1, tiled=True)
    own = lax.psum_scatter(full, "narrow", scatter_dimension=1, tiled=True)
    own = own.reshape(STEPS, local_rolls, -1, query_cols + 2 * key_cols)
    query_own = own[..., :query_cols].reshape(STEPS, local_rolls, heads_local, HD)
    key_own = own[..., query_cols : query_cols + key_cols].reshape(STEPS, local_rolls, kv_local, HD)
    value_own = own[..., query_cols + key_cols :].reshape(STEPS, local_rolls, kv_local, HD)
    step_ids = jnp.arange(STEPS, dtype=jnp.int32)
    angles = angles_for(lengths[None, :] + step_ids[:, None], HD)[:, :, None, :]
    queries = rotate(query_own, angles).astype(jnp.bfloat16)
    keys_now = rotate(key_own, angles).astype(jnp.bfloat16)
    values_now = value_own.astype(jnp.bfloat16)
    keys_now = jnp.transpose(keys_now, (1, 2, 0, 3))
    values_now = jnp.transpose(values_now, (1, 2, 0, 3))
    grouped = queries.reshape(STEPS, local_rolls, kv_local, group_size, HD)
    grouped = jnp.transpose(grouped, (1, 2, 0, 3, 4)).reshape(
        local_rolls, kv_local, STEPS * group_size, HD
    )
    old_scores = (
        jnp.einsum("rkqd,rkcd->rkqc", grouped, k_cache, preferred_element_type=jnp.float32)
        * score_scale
    )
    old_scores = jnp.where(cache_live[:, None, None, :], old_scores, -jnp.inf)
    new_scores = (
        jnp.einsum("rkqd,rktd->rkqt", grouped, keys_now, preferred_element_type=jnp.float32)
        * score_scale
    )
    query_step = jnp.arange(STEPS * group_size, dtype=jnp.int32) // group_size
    new_live = step_ids[None, :] <= query_step[:, None]
    new_scores = jnp.where(new_live[None, None], new_scores, -jnp.inf)
    largest = jnp.maximum(
        jnp.max(old_scores, axis=-1, keepdims=True), jnp.max(new_scores, axis=-1, keepdims=True)
    )
    old_weights = jnp.exp(old_scores - largest)
    new_weights = jnp.exp(new_scores - largest)
    total = jnp.sum(old_weights, axis=-1, keepdims=True) + jnp.sum(
        new_weights, axis=-1, keepdims=True
    )
    mixed_heads = jnp.einsum(
        "rkqc,rkcd->rkqd",
        (old_weights / total).astype(jnp.bfloat16),
        v_cache,
        preferred_element_type=jnp.float32,
    ) + jnp.einsum(
        "rkqt,rktd->rkqd",
        (new_weights / total).astype(jnp.bfloat16),
        values_now,
        preferred_element_type=jnp.float32,
    )
    mixed_heads = mixed_heads.astype(jnp.bfloat16).reshape(
        local_rolls, kv_local, STEPS, group_size, HD
    )
    mixed_heads = jnp.transpose(mixed_heads, (2, 0, 1, 3, 4)).reshape(
        STEPS * local_rolls, heads_local * HD
    )
    out_part = jnp.dot(
        lax.all_gather(mixed_heads, "wide", axis=0, tiled=True),
        w_out,
        preferred_element_type=jnp.float32,
    )
    out_full = lax.all_to_all(
        out_part.astype(jnp.bfloat16), "wide", split_axis=0, concat_axis=1, tiled=True
    )
    out_own = lax.psum_scatter(out_full, "narrow", scatter_dimension=1, tiled=True).astype(
        jnp.float32
    )
    residual = tokens + out_own
    ffn_sums = lax.psum(jnp.sum(residual * residual, axis=1), "narrow")
    normed_ffn = scale_rows(residual, ffn_sums, gain_ffn, full_width)
    block_rows = lax.all_gather(normed_ffn, "wide", axis=0, tiled=True)
    lifted = jnp.concatenate(
        [
            jnp.dot(block_rows, w_gate, preferred_element_type=jnp.float32),
            jnp.dot(block_rows, w_up, preferred_element_type=jnp.float32),
        ],
        axis=1,
    )
    lifted_total = lax.psum(lifted.astype(jnp.bfloat16), "narrow").astype(jnp.float32)
    hidden = (jax.nn.silu(lifted_total[:, :ffn_cols]) * lifted_total[:, ffn_cols:]).astype(
        jnp.bfloat16
    )
    down_own = lax.psum_scatter(
        jnp.dot(hidden, w_down, preferred_element_type=jnp.float32).astype(jnp.bfloat16),
        "wide",
        scatter_dimension=0,
        tiled=True,
    ).astype(jnp.float32)
    result = (residual + down_own).reshape(STEPS, local_rolls, half_width)
    return (result, keys_now, values_now)


def solution(mesh):
    placed = (
        P(None, ("group", "wide"), "narrow"),
        P(("group", "wide")),
        P(("group", "wide"), "narrow", None, None),
        P(("group", "wide"), "narrow", None, None),
        P("narrow"),
        P("narrow"),
        P("narrow", "wide"),
        P("narrow", "wide"),
        P("narrow", "wide"),
        P("narrow", "wide"),
        P("narrow", "wide"),
        P("narrow", "wide"),
        P("wide", "narrow"),
    )
    return jax.shard_map(
        shards,
        mesh=mesh,
        in_specs=placed,
        out_specs=(
            P(None, ("group", "wide"), "narrow"),
            P(("group", "wide"), "narrow", None, None),
            P(("group", "wide"), "narrow", None, None),
        ),
        check_vma=False,
    )
```

profile of v0, /device:TPU:0, one launch (start us, length us, event | category | flops | bytes accessed | tf_op | source)
XLA Modules:
  0.0 286.4 jit_solution(17484352957417439058)
XLA Ops:
  7.2 1.2 multiply_reduce_fusion.1
  8.4 0.9 reshape.139
  9.4 2.6 psum.21
  12.7 33.5 %all_gather.9 = bf16[128,2560]{1,0:T(8,128)(2,1)S(1)} all-gather(bf16[16,2560]{1,0:T(8,128)(2,1)S(1)} %multiply_convert_fusion.1), channel_id=1, replica_groups=mesh['group'=2,'wide'=8,'narrow'=2] {'wide'}, dimensions={0}, use_global_device_ids=true | all-gather | bytes 737280 | tf_op jit(solution)/shard_map/all_gather | solution.py:70
  46.2 1.4 fusion.22
  47.6 1.4 fusion.21
  49.8 15.1 %all_to_all.38 = f32[8,16,896]{2,1,0:T(8,128)S(1)} all-to-all(f32[8,16,896]{2,1,0:T(8,128)S(1)} %bitcast.40), channel_id=1, replica_groups=mesh['group'=2,'wide'=8,'narrow'=2] {'wide'}, dimensions={0} | all-to-all | bytes 917504 | tf_op jit(solution)/shard_map/all_to_all | solution.py:79
  67.2 5.3 %reduce-scatter.4.cloned.1.call-done = f32[16,3584]{1,0:T(8,128)} async-done(((f32[16,7168]{1,0:T(8,128)}), f32[16,3584]{1,0:T(8,128)}) %reduce-scatter.4.cloned.1.call-update) | async-done | bytes 229392 | tf_op jit(solution)/shard_map/reduce_scatter | solution.py:80
  72.5 1.7 reshape.133
  74.9 0.9 fusion.17
  75.9 1.6 slice.36
  77.5 1.7 reshape.134
  79.1 1.3 subtract_convert_fusion
  82.2 2.4 fusion.18
  86.4 1.0 reshape.137
  87.4 32.2 %all_gather.10 = bf16[128,2560]{1,0:T(8,128)(2,1)S(1)} all-gather(bf16[16,2560]{1,0:T(8,128)(2,1)S(1)} %reshape.137), channel_id=1, replica_groups=mesh['group'=2,'wide'=8,'narrow'=2] {'wide'}, dimensions={0}, use_global_device_ids=true | all-gather | bytes 737280 | tf_op jit(solution)/shard_map/all_gather | solution.py:134
  119.6 2.6 convolution_convert_fusion.3
  122.2 12.8 %all_to_all.39 = bf16[8,16,640]{2,1,0:T(8,128)(2,1)S(1)} all-to-all(bf16[8,16,640]{2,1,0:T(8,128)(2,1)S(1)} %bitcast.42), channel_id=1, replica_groups=mesh['group'=2,'wide'=8,'narrow'=2] {'wide'}, dimensions={0} | all-to-all | bytes 327680 | tf_op jit(solution)/shard_map/all_to_all | solution.py:138
  135.8 5.5 %reduce-scatter.6.cloned.1.call-done = bf16[16,2560]{1,0:T(8,128)(2,1)} async-done(((bf16[16,5120]{1,0:T(8,128)(2,1)}), bf16[16,2560]{1,0:T(8,128)(2,1)}) %reduce-scatter.6.cloned.1.call-update) | async-done | bytes 81936 | tf_op jit(solution)/shard_map/reduce_scatter | solution.py:141
  141.2 1.0 multiply_reduce_fusion
  142.2 2.5 psum.22
  144.7 1.0 multiply_convert_fusion
  145.7 32.3 %all_gather.11 = bf16[128,2560]{1,0:T(8,128)(2,1)S(1)} all-gather(bf16[16,2560]{1,0:T(8,128)(2,1)S(1)} %multiply_convert_fusion), channel_id=1, replica_groups=mesh['group'=2,'wide'=8,'narrow'=2] {'wide'}, dimensions={0}, use_global_device_ids=true | all-gather | bytes 737280 | tf_op jit(solution)/shard_map/all_gather | solution.py:147
  178.0 5.1 %convolution_convert_fusion.1 = bf16[128,1792]{1,0:T(8,128)(2,1)S(1)} fusion(bf16[128,2560]{1,0:T(8,128)(2,1)S(1)} %all_gather.11, bf16[2560,1792]{1,0:T(8,128)(2,1)} %param.24), kind=kOutput, calls=%fused_computation.1 | convolution fusion | flops 1174634496 | bytes 10289152 | tf_op jit(solution)/shard_map/dot_general | solution.py:151
  183.2 1.4 convolution_convert_fusion.2
  184.6 1.0 pad_maximum_fusion
  185.7 20.3 %all-reduce.2.cloned.1.call-done = bf16[128,3584]{1,0:T(8,128)(2,1)} async-done(((bf16[128,3584]{1,0:T(8,128)(2,1)}), bf16[128,3584]{1,0:T(8,128)(2,1)}) %all-reduce.2.cloned.1.call-update) | async-done | bytes 917520 | tf_op jit(solution)/shard_map/psum | solution.py:155
  206.0 1.4 convert_element_type.73
  207.3 6.0 %convolution_convert_fusion = bf16[128,2560]{1,0:T(8,128)(2,1)} fusion(bf16[1792,2560]{1,0:T(8,128)(2,1)} %param.25, f32[128,3584]{1,0:T(8,128)S(1)} %convert_element_type.73), kind=kOutput, calls=%fused_computation | convolution fusion | flops 1176109056 | bytes 11665408 | tf_op jit(solution)/shard_map/dot_general | solution.py:160
  213.3 63.4 %reduce-scatter.8.cloned.1.call-done = bf16[16,2560]{1,0:T(8,128)(2,1)} async-done(((bf16[128,2560]{1,0:T(8,128)(2,1)}), bf16[16,2560]{1,0:T(8,128)(2,1)}) %reduce-scatter.8.cloned.1.call-update) | async-done | bytes 81936 | tf_op jit(solution)/shard_map/reduce_scatter | solution.py:159
  276.7 1.6 convert_add_fusion
  278.3 1.6 reshape.138
  (63 shorter events, 8.9 us)
Async XLA Ops:
  7.2 41.9 %copy-start = (bf16[2560,640]{1,0:T(8,128)(2,1)S(1)}, bf16[2560,640]{1,0:T(8,128)(2,1)}, u32[]{:S(2)}) copy-start(bf16[2560,640]{1,0:T(8,128)(2,1)} %param.19) | copy-start | bytes 9830404
  7.2 65.3 %reduce-scatter.4.cloned.1.call-start = ((), (), s32[]{:S(2)}) async-start(), calls=%async_computation.5 | async-start | bytes 688128 | tf_op jit(solution)/shard_map/reduce_scatter | solution.py:80
  49.0 16.7 %copy-start.5 = (s32[4]{0:T(128)S(1)}, s32[4]{0:T(128)}, u32[]{:S(2)}) copy-start(s32[4]{0:T(128)} %param.14) | copy-start | bytes 52
  65.7 75.5 %reduce-scatter.6.cloned.1.call-start = ((), (), s32[]{:S(2)}) async-start(), calls=%async_computation.6 | async-start | bytes 245760 | tf_op jit(solution)/shard_map/reduce_scatter | solution.py:141
  79.1 6.1 %copy-start.6 = (bf16[4,4,384,128]{3,2,1,0:T(8,128)(2,1)S(1)}, bf16[4,4,384,128]{3,2,1,0:T(8,128)(2,1)}, u32[]{:S(2)}) copy-start(bf16[4,4,384,128]{3,2,1,0:T(8,128)(2,1)} %param.16) | copy-start | bytes 4718596
  80.8 0.6 copy-start.3
  80.8 4.9 %copy-start.2 = (bf16[4,4,4,128]{3,2,1,0:T(4,128)(2,1)}, bf16[4,4,4,128]{3,2,1,0:T(4,128)(2,1)S(1)}, u32[]{:S(2)}) copy-start(bf16[4,4,4,128]{3,2,1,0:T(4,128)(2,1)S(1)} %get-tuple-element.15) | copy-start | bytes 49156
  85.7 50.1 %copy-start.4 = (bf16[2560]{0:T(1024)(128)(2,1)S(1)}, bf16[2560]{0:T(1024)(128)(2,1)}, u32[]{:S(2)}) copy-start(bf16[2560]{0:T(1024)(128)(2,1)} %param.18) | copy-start | bytes 15364
  135.7 70.3 %all-reduce.2.cloned.1.call-start = ((), (), s32[]{:S(2)}) async-start(), calls=%async_computation.7 | async-start | bytes 1835008 | tf_op jit(solution)/shard_map/psum | solution.py:155
  145.7 37.5 %slice-start = ((s8[9175040]{0:T(1024)(128)(4,1)}), s8[4194304]{0:T(1024)(128)(4,1)S(1)}, s32[]{:S(2)}) async-start(s8[9175040]{0:T(1024)(128)(4,1)} %bitcast.37), calls=%async_computation.9 | async-start | bytes 8388608
  178.0 5.1 %slice-start.1 = ((s8[9175040]{0:T(1024)(128)(4,1)}), s8[4194304]{0:T(1024)(128)(4,1)S(1)}, s32[]{:S(2)}) async-start(s8[9175040]{0:T(1024)(128)(4,1)} %bitcast.37), calls=%async_computation.10 | async-start | bytes 8388608
  178.0 5.1 %slice-start.2 = ((s8[9175040]{0:T(1024)(128)(4,1)}), s8[786432]{0:T(1024)(128)(4,1)S(1)}, s32[]{:S(2)}) async-start(s8[9175040]{0:T(1024)(128)(4,1)} %bitcast.37), calls=%async_computation.11 | async-start | bytes 1572864
  185.6 91.1 %reduce-scatter.8.cloned.1.call-start = ((), (), s32[]{:S(2)}) async-start(), calls=%async_computation.8 | async-start | bytes 737280 | tf_op jit(solution)/shard_map/reduce_scatter | solution.py:159
  207.3 69.4 %copy-start.1 = (bf16[16,2560]{1,0:T(8,128)(2,1)S(1)}, bf16[16,2560]{1,0:T(8,128)(2,1)}, u32[]{:S(2)}) copy-start(bf16[16,2560]{1,0:T(8,128)(2,1)} %reduce-scatter.6.cloned.1.call-done) | copy-start | bytes 245764
Sparse Core Ops, SparseCore 0:
  65.8 6.5 reduce-scatter.3
  135.8 5.3 reduce-scatter.5
  185.8 20.1 all-reduce.1
  213.4 63.2 reduce-scatter.7
where the time goes:
time: 287 us; the launch traced here: 286 us
  blocking collectives  131 us (46%)
  waiting for transfers between devices  94.5 us (33%)
  matrix products  22.5 us (8%)
  between operations  14.1 us (5%)
  local copies, waits for them, and re-layouts  13.2 us (5%)
  other arithmetic  11.1 us (4%)
    reduce_scatter x1, waiting for transfers between devices, shards(): lax.psum_scatter(jnp.dot(hidden, w_down, preferred_element_type=jnp.float...  63.4 us
    all_gather x1, blocking collectives, shards(): rows_all = lax.all_gather(normed, 'wide', axis=0, tiled=True)  33.5 us
    all_gather x1, blocking collectives, shards(): block_rows = lax.all_gather(normed_ffn, 'wide', axis=0, tiled=True)  32.3 us
    all_gather x1, blocking collectives, shards(): lax.all_gather(mixed_heads, 'wide', axis=0, tiled=True)  32.2 us
    psum x1, waiting for transfers between devices, shards(): lax.psum(lifted.astype(jnp.bfloat16), 'narrow').astype(jnp.float32)  20.3 us
    all_to_all x1, blocking collectives, shards(): lax.all_to_all(partial, 'wide', split_axis=0, concat_axis=1, tiled=True)  15.1 us
    all_to_all x1, blocking collectives, shards(): lax.all_to_all(out_part.astype(jnp.bfloat16), 'wide', split_axis=0, conca...  12.8 us
    dot_general x1, matrix products, shards(): jnp.dot(hidden, w_down, preferred_element_type=jnp.float32)  5.97 us
  transfers between devices with their start and end apart: 4, of which 4 were waited for; matrix products, arithmetic and copies ran while one was open for 0% of the time, Pallas kernels for 0%

commit v1 on v0

--- a/solution.py
+++ b/solution.py
@@ -3,6 +3,8 @@
 import jax
 import jax.numpy as jnp
 from jax import lax
+from jax.experimental import pallas as pl
+from jax.experimental.pallas import tpu as pltpu
 from jax.sharding import PartitionSpec as P
 
 HQ = 40
@@ -35,6 +37,336 @@
 def scale_rows(tokens, row_sums, gain_row, full_width):
     factor = lax.rsqrt(row_sums / full_width + norm_eps)
     return (tokens * factor[:, None] * gain_row.astype(jnp.float32)).astype(jnp.bfloat16)
+
+
+def ring_place(device):
+    row, side = device // 2, device % 2
+    return row + side * (7 - 2 * row)
+
+
+def ring_device(place):
+    side = place // 4
+    return 2 * (place + side * (7 - 2 * place)) + side
+
+
+def greet_group():
+    wide, narrow = lax.axis_index("wide"), lax.axis_index("narrow")
+    barrier = pltpu.get_barrier_semaphore()
+    for step in range(16):
+        if step != 0:
+            other_wide = (wide + step // 2) % 8
+            other_narrow = (narrow + step % 2) % 2
+            pl.semaphore_signal(
+                barrier,
+                inc=1,
+                device_id={"wide": other_wide, "narrow": other_narrow},
+                device_id_type=pl.DeviceIdType.MESH,
+            )
+    pl.semaphore_wait(barrier, 15)
+
+
+def send(source, target, send_sem, recv_sem, wide, narrow):
+    return pltpu.make_async_remote_copy(
+        src_ref=source,
+        dst_ref=target,
+        send_sem=send_sem,
+        recv_sem=recv_sem,
+        device_id={"wide": wide, "narrow": narrow},
+        device_id_type=pl.DeviceIdType.MESH,
+    )
+
+
+def ring_gather(blocks, send_sems, recv_sems):
+    wide, narrow = lax.axis_index("wide"), lax.axis_index("narrow")
+    place = ring_place(wide)
+    right = ring_device((place + 1) % 8)
+    left = ring_device((place + 7) % 8)
+    half = blocks.shape[2] // 2
+    ups, downs = [], []
+    for hop in range(4):
+        up_owner = ring_device((place + 8 - hop) % 8)
+        down_owner = ring_device((place + hop) % 8)
+        up_block, down_block = blocks.at[up_owner], blocks.at[down_owner]
+        if hop == 3:
+            up_block = blocks.at[up_owner, :, pl.ds(0, half)]
+            down_block = blocks.at[down_owner, :, pl.ds(half, half)]
+        if hop > 0:
+            ups[-1].wait_recv()
+        ups.append(
+            send(up_block, up_block, send_sems.at[hop], recv_sems.at[hop], right, narrow)
+        )
+        ups[-1].start()
+        if hop > 0:
+            downs[-1].wait_recv()
+        downs.append(
+            send(down_block, down_block, send_sems.at[4 + hop], recv_sems.at[4 + hop], left, narrow)
+        )
+        downs[-1].start()
+    ups[-1].wait_recv()
+    downs[-1].wait_recv()
+    for copy in ups + downs:
+        copy.wait_send()
+
+
+def norm_own(tokens, gain_ref, sums_out, sums_in, send_sem, recv_sem, full_width):
+    wide, narrow = lax.axis_index("wide"), lax.axis_index("narrow")
+    own_sums = jnp.sum(tokens * tokens, axis=1, keepdims=True)
+    sums_out[...] = jnp.broadcast_to(own_sums, sums_out.shape)
+    copy = send(sums_out, sums_in, send_sem, recv_sem, wide, 1 - narrow)
+    copy.start()
+    copy.wait()
+    row_sums = own_sums + sums_in[:, 0:1]
+    factor = lax.rsqrt(row_sums / full_width + norm_eps)
+    return (tokens * factor * gain_ref[...].astype(jnp.float32)).astype(jnp.bfloat16)
+
+
+def send_to_owners(parts, arrived, send_sems, recv_sems):
+    wide, narrow = lax.axis_index("wide"), lax.axis_index("narrow")
+    column_half = wide // 4
+    my_slot = (wide % 4) * 2 + narrow
+    keeps_own = column_half == narrow
+    copies = []
+    for step in range(8):
+        owner = (wide + step) % 8
+        copies.append(
+            send(
+                parts.at[owner],
+                arrived.at[my_slot],
+                send_sems.at[step],
+                recv_sems.at[my_slot],
+                owner,
+                column_half,
+            )
+        )
+    for copy in copies[1:]:
+        copy.start()
+    pl.when(jnp.logical_not(keeps_own))(copies[0].start)
+
+    @pl.when(keeps_own)
+    def _():
+        arrived[my_slot] = parts[wide]
+
+    for slot in range(8):
+        comes = jnp.logical_or(wide != narrow * 4 + slot // 2, narrow != slot % 2)
+        landed = send(
+            parts.at[0],
+            arrived.at[slot],
+            send_sems.at[0],
+            recv_sems.at[slot],
+            wide,
+            1 - narrow,
+        )
+        pl.when(comes)(landed.wait_recv)
+    for copy in copies[1:]:
+        copy.wait_send()
+    pl.when(jnp.logical_not(keeps_own))(copies[0].wait_send)
+
+
+def project_kernel(
+    tokens_ref, gain_ref, w_query, w_key, w_value, own_ref,
+    weights, blocks, parts, arrived, sums_out, sums_in,
+    load_sems, ring_send, ring_recv, part_send, part_recv, sums_send, sums_recv,
+):
+    query_cols, key_cols = w_query.shape[1], w_key.shape[1]
+    places = [(0, query_cols), (query_cols, key_cols), (query_cols + key_cols, key_cols)]
+    loads = [
+        pltpu.make_async_copy(matrix, weights.at[:, pl.ds(at, size)], load_sems.at[i])
+        for i, (matrix, (at, size)) in enumerate(zip((w_query, w_key, w_value), places))
+    ]
+    for load in loads:
+        load.start()
+    greet_group()
+    half_width = tokens_ref.shape[1]
+    tokens = tokens_ref[...].astype(jnp.float32)
+    normed = norm_own(
+        tokens, gain_ref, sums_out, sums_in, sums_send.at[0], sums_recv.at[0], 2 * half_width
+    )
+    blocks[lax.axis_index("wide")] = normed
+    ring_gather(blocks, ring_send, ring_recv)
+    for load in loads:
+        load.wait()
+    rows = blocks[...].reshape(-1, half_width)
+    sums = jnp.dot(rows, weights[...], preferred_element_type=jnp.float32)
+    parts[...] = sums.reshape(parts.shape)
+    send_to_owners(parts, arrived, part_send, part_recv)
+    for peer in range(4):
+        own_ref[peer] = arrived[2 * peer] + arrived[2 * peer + 1]
+
+
+def finish_kernel(
+    mixed_ref, tokens_ref, gain_ref, w_out, w_gate, w_up, w_down, result_ref,
+    out_weights, gate_weights, up_weights, down_weights,
+    mixed_blocks, out_parts, out_arrived, residual, normed_blocks, sums_out, sums_in,
+    lifted, lifted_out, lifted_in, hidden, down_parts, down_arrived,
+    load_sems, mixed_send, mixed_recv, part_send, part_recv, sums_send, sums_recv,
+    normed_send, normed_recv, lifted_send, lifted_recv, down_send, down_recv,
+):
+    wide, narrow = lax.axis_index("wide"), lax.axis_index("narrow")
+    half_width = tokens_ref.shape[1]
+    loads = [
+        pltpu.make_async_copy(matrix, place, load_sems.at[i])
+        for i, (matrix, place) in enumerate(
+            [(w_out, out_weights), (w_gate, gate_weights), (w_up, up_weights), (w_down, down_weights)]
+        )
+    ]
+    for load in loads:
+        load.start()
+    greet_group()
+    mixed_blocks[wide] = mixed_ref[...]
+    ring_gather(mixed_blocks, mixed_send, mixed_recv)
+    loads[0].wait()
+    out_sums = jnp.dot(
+        mixed_blocks[...].reshape(-1, half_width),
+        out_weights[...],
+        preferred_element_type=jnp.float32,
+    )
+    out_parts[...] = out_sums.astype(jnp.bfloat16).reshape(out_parts.shape)
+    send_to_owners(out_parts, out_arrived, part_send, part_recv)
+    out_cols = out_weights.shape[1]
+    for peer in range(4):
+        columns = pl.ds(peer * out_cols, out_cols)
+        residual[:, columns] = (
+            tokens_ref[:, columns].astype(jnp.float32)
+            + out_arrived[2 * peer].astype(jnp.float32)
+            + out_arrived[2 * peer + 1].astype(jnp.float32)
+        )
+    normed_blocks[wide] = norm_own(
+        residual[...], gain_ref, sums_out, sums_in, sums_send.at[0], sums_recv.at[0], 2 * half_width
+    )
+    ring_gather(normed_blocks, normed_send, normed_recv)
+    loads[1].wait()
+    loads[2].wait()
+    chunks, chunk = lifted.shape[0], lifted.shape[3]
+
+    def lifted_copy(i):
+        return send(
+            lifted_out.at[i], lifted_in.at[i], lifted_send.at[i], lifted_recv.at[i], wide, 1 - narrow
+        )
+
+    def lift(i, carry):
+        columns = pl.ds(pl.multiple_of(i * chunk, chunk), chunk)
+        rows = normed_blocks[...].reshape(-1, half_width)
+        for side, weights in enumerate((gate_weights, up_weights)):
+            sums = jnp.dot(rows, weights[:, columns], preferred_element_type=jnp.float32)
+            lifted[i, side] = sums
+            lifted_out[i, side] = sums.astype(jnp.bfloat16)
+        lifted_copy(i).start()
+        return carry
+
+    lax.fori_loop(0, chunks, lift, 0)
+
+    def activate(i, carry):
+        columns = pl.ds(pl.multiple_of(i * chunk, chunk), chunk)
+        lifted_copy(i).wait()
+        gate = lifted[i, 0] + lifted_in[i, 0].astype(jnp.float32)
+        up = lifted[i, 1] + lifted_in[i, 1].astype(jnp.float32)
+        hidden[:, columns] = (gate / (1.0 + jnp.exp(-gate)) * up).astype(jnp.bfloat16)
+        return carry
+
+    lax.fori_loop(0, chunks, activate, 0)
+    loads[3].wait()
+    down_chunk = 512
+
+    def lower(i, carry):
+        columns = pl.ds(pl.multiple_of(i * down_chunk, down_chunk), down_chunk)
+        sums = jnp.dot(hidden[...], down_weights[:, columns], preferred_element_type=jnp.float32)
+        down_parts[:, :, columns] = sums.astype(jnp.bfloat16).reshape(8, -1, down_chunk)
+        return carry
+
+    lax.fori_loop(0, half_width // down_chunk, lower, 0)
+    copies = []
+    for step in range(1, 8):
+        owner = (wide + step) % 8
+        copies.append(
+            send(
+                down_parts.at[owner],
+                down_arrived.at[step - 1],
+                down_send.at[step - 1],
+                down_recv.at[step - 1],
+                owner,
+                narrow,
+            )
+        )
+        copies[-1].start()
+    total = residual[...] + down_parts[wide].astype(jnp.float32)
+    for step, copy in enumerate(copies):
+        copy.wait_recv()
+        total = total + down_arrived[step].astype(jnp.float32)
+    result_ref[...] = total
+    for copy in copies:
+        copy.wait_send()
+
+
+def in_vmem():
+    return pl.BlockSpec(memory_space=pltpu.VMEM)
+
+
+def in_place():
+    return pl.BlockSpec(memory_space=pl.ANY)
+
+
+def project(tokens, gain, w_query, w_key, w_value):
+    count, half_width = tokens.shape
+    columns = w_query.shape[1] + 2 * w_key.shape[1]
+    dma = pltpu.SemaphoreType.DMA
+    return pl.pallas_call(
+        project_kernel,
+        out_shape=jax.ShapeDtypeStruct((4, count, columns), jnp.float32),
+        in_specs=[in_vmem()] * 2 + [in_place()] * 3,
+        out_specs=in_vmem(),
+        scratch_shapes=[
+            pltpu.VMEM((half_width, columns), jnp.bfloat16),
+            pltpu.VMEM((8, count, half_width), jnp.bfloat16),
+            pltpu.VMEM((8, count, columns), jnp.float32),
+            pltpu.VMEM((8, count, columns), jnp.float32),
+            pltpu.VMEM((count, 128), jnp.float32),
+            pltpu.VMEM((count, 128), jnp.float32),
+            dma((3,)), dma((8,)), dma((8,)), dma((8,)), dma((8,)), dma((1,)), dma((1,)),
+        ],
+        compiler_params=pltpu.CompilerParams(
+            collective_id=0, has_side_effects=True, vmem_limit_bytes=32 * 2**20
+        ),
+        name="project",
+    )(tokens, gain.reshape(1, -1), w_query, w_key, w_value)
+
+
+def finish(mixed, tokens, gain, w_out, w_gate, w_up, w_down):
+    count, half_width = tokens.shape
+    out_cols, ffn_cols = w_out.shape[1], w_gate.shape[1]
+    chunk = 256
+    chunks = ffn_cols // chunk
+    dma = pltpu.SemaphoreType.DMA
+    return pl.pallas_call(
+        finish_kernel,
+        out_shape=jax.ShapeDtypeStruct((count, half_width), jnp.float32),
+        in_specs=[in_vmem()] * 3 + [in_place()] * 4,
+        out_specs=in_vmem(),
+        scratch_shapes=[
+            pltpu.VMEM(w_out.shape, jnp.bfloat16),
+            pltpu.VMEM(w_gate.shape, jnp.bfloat16),
+            pltpu.VMEM(w_up.shape, jnp.bfloat16),
+            pltpu.VMEM(w_down.shape, jnp.bfloat16),
+            pltpu.VMEM((8, count, half_width), jnp.bfloat16),
+            pltpu.VMEM((8, count, out_cols), jnp.bfloat16),
+            pltpu.VMEM((8, count, out_cols), jnp.bfloat16),
+            pltpu.VMEM((count, half_width), jnp.float32),
+            pltpu.VMEM((8, count, half_width), jnp.bfloat16),
+            pltpu.VMEM((count, 128), jnp.float32),
+            pltpu.VMEM((count, 128), jnp.float32),
+            pltpu.VMEM((chunks, 2, 8 * count, chunk), jnp.float32),
+            pltpu.VMEM((chunks, 2, 8 * count, chunk), jnp.bfloat16),
+            pltpu.VMEM((chunks, 2, 8 * count, chunk), jnp.bfloat16),
+            pltpu.VMEM((8 * count, ffn_cols), jnp.bfloat16),
+            pltpu.VMEM((8, count, half_width), jnp.bfloat16),
+            pltpu.VMEM((7, count, half_width), jnp.bfloat16),
+            dma((4,)), dma((8,)), dma((8,)), dma((8,)), dma((8,)), dma((1,)), dma((1,)),
+            dma((8,)), dma((8,)), dma((chunks,)), dma((chunks,)), dma((7,)), dma((7,)),
+        ],
+        compiler_params=pltpu.CompilerParams(
+            collective_id=1, has_side_effects=True, vmem_limit_bytes=56 * 2**20
+        ),
+        name="finish",
+    )(mixed, tokens, gain.reshape(1, -1), w_out, w_gate, w_up, w_down)
 
 
 def shards(
@@ -64,20 +396,28 @@
     ffn_cols = w_gate.shape[1]
     score_scale = 1.0 / math.sqrt(HD)
     cache_live = jnp.arange(cache_len, dtype=jnp.int32)[None, :] < lengths[:, None]
-    tokens = embeds.reshape(STEPS * local_rolls, half_width).astype(jnp.float32)
-    attn_sums = lax.psum(jnp.sum(tokens * tokens, axis=1), "narrow")
-    normed = scale_rows(tokens, attn_sums, gain_attn, full_width)
-    rows_all = lax.all_gather(normed, "wide", axis=0, tiled=True)
-    partial = jnp.concatenate(
-        [
-            jnp.dot(rows_all, w_query, preferred_element_type=jnp.float32),
-            jnp.dot(rows_all, w_key, preferred_element_type=jnp.float32),
-            jnp.dot(rows_all, w_value, preferred_element_type=jnp.float32),
-        ],
-        axis=1,
-    )
-    full = lax.all_to_all(partial, "wide", split_axis=0, concat_axis=1, tiled=True)
-    own = lax.psum_scatter(full, "narrow", scatter_dimension=1, tiled=True)
+    own_rows = embeds.reshape(STEPS * local_rolls, half_width)
+    tokens = own_rows.astype(jnp.float32)
+    by_kernel = (
+        lax.axis_size("wide") == 8 and query_cols % 128 == 0 and ffn_cols % 256 == 0
+    )
+    if by_kernel:
+        own = project(own_rows, gain_attn, w_query, w_key, w_value)
+        own = jnp.transpose(own, (1, 0, 2))
+    else:
+        attn_sums = lax.psum(jnp.sum(tokens * tokens, axis=1), "narrow")
+        normed = scale_rows(tokens, attn_sums, gain_attn, full_width)
+        rows_all = lax.all_gather(normed, "wide", axis=0, tiled=True)
+        partial = jnp.concatenate(
+            [
+                jnp.dot(rows_all, w_query, preferred_element_type=jnp.float32),
+                jnp.dot(rows_all, w_key, preferred_element_type=jnp.float32),
+                jnp.dot(rows_all, w_value, preferred_element_type=jnp.float32),
+            ],
+            axis=1,
+        )
+        full = lax.all_to_all(partial, "wide", split_axis=0, concat_axis=1, tiled=True)
+        own = lax.psum_scatter(full, "narrow", scatter_dimension=1, tiled=True)
     own = own.reshape(STEPS, local_rolls, -1, query_cols + 2 * key_cols)
     query_own = own[..., :query_cols].reshape(STEPS, local_rolls, heads_local, HD)
     key_own = own[..., query_cols : query_cols + key_cols].reshape(STEPS, local_rolls, kv_local, HD)
@@ -130,6 +470,9 @@
     mixed_heads = jnp.transpose(mixed_heads, (2, 0, 1, 3, 4)).reshape(
         STEPS * local_rolls, heads_local * HD
     )
+    if by_kernel:
+        result = finish(mixed_heads, own_rows, gain_ffn, w_out, w_gate, w_up, w_down)
+        return (result.reshape(STEPS, local_rolls, half_width), keys_now, values_now)
     out_part = jnp.dot(
         lax.all_gather(mixed_heads, "wide", axis=0, tiled=True),
         w_out,

time: 287 us -> 108 us (0.38)
  the two profiles are of different devices: /device:TPU:0 before, /device:TPU:13 now
where the time goes in v1:
time: 108 us
  Pallas kernels  94.4 us (87%)
  local copies, waits for them, and re-layouts  9.34 us (9%)
  matrix products  1.92 us (2%)
    pallas_call x1, Pallas kernels, finish(): pl.pallas_call(finish_kernel, out_shape=jax.ShapeDtypeStruct((count, half...  64.2 us
    pallas_call x1, Pallas kernels, project(): pl.pallas_call(project_kernel, out_shape=jax.ShapeDtypeStruct((4, count,...  30.2 us
    unnamed x21, local copies, waits for them, and re-layouts  4.2 us

profile of v1, /device:TPU:13, one launch (start us, length us, event | category | flops | bytes accessed | tf_op | source)
XLA Modules:
  0.0 107.6 jit_solution(9293555719162560155)
XLA Ops:
  0.6 0.0 copy-start
  0.6 1.0 reshape.128.tokens_ref
  1.7 0.0 copy-start.2
  1.7 0.7 reshape.129.gain_ref
  2.4 1.9 %copy-done.1 = bf16[2560,640]{1,0:T(8,128)(2,1)S(1)} copy-done((bf16[2560,640]{1,0:T(8,128)(2,1)S(1)}, bf16[2560,640]{1,0:T(8,128)(2,1)}, u32[]{:S(2)}) %copy-start.1) | copy-done | bytes 3276824
  4.3 1.1 %copy-done.3 = bf16[2560,128]{1,0:T(8,128)(2,1)S(1)} copy-done((bf16[2560,128]{1,0:T(8,128)(2,1)S(1)}, bf16[2560,128]{1,0:T(8,128)(2,1)}, u32[]{:S(2)}) %copy-start.3) | copy-done | bytes 655384
  5.4 1.1 %copy-done.4 = bf16[2560,128]{1,0:T(8,128)(2,1)S(1)} copy-done((bf16[2560,128]{1,0:T(8,128)(2,1)S(1)}, bf16[2560,128]{1,0:T(8,128)(2,1)}, u32[]{:S(2)}) %copy-start.4) | copy-done | bytes 655384
  6.5 30.2 %project.1 = f32[4,16,896]{2,1,0:T(8,128)S(1)} custom-call(bf16[16,2560]{1,0:T(8,128)(2,1)S(1)} %reshape.128.tokens_ref, bf16[1,2560]{1,0:T(2,128)(2,1)S(1)} %reshape.129.gain_ref, bf16[2560,640]{1,0:T(8,128)(2,1)S(1)} %copy-done.1, bf16[2560,128]{1,0:T(8,128)(2,1)S(1)} %copy-done.3, bf16[2560,128]{1,0:T(8,128)(2,1)S(1)} %copy-done.4), custom_call_target="tpu_custom_call" | custom-call | tf_op jit(solution)/shard_map/project/pallas_call | solution.py:312
  36.7 0.0 copy-done.2
  36.7 0.1 reshape.130
  36.8 0.1 fusion.13
  36.9 0.0 copy-done.8
  36.9 0.1 add_convert_fusion.2
  36.9 0.1 multiply_cosine_fusion
  37.1 0.1 fusion.10
  37.2 0.0 copy-start.6
  37.3 0.0 copy-start.5
  37.3 0.1 copy.35
  37.4 0.1 reshape.131
  37.5 0.1 subtract_convert_fusion
  37.7 0.1 maximum_bitcast_fusion
  37.9 0.2 fusion.15
  38.1 0.1 iota_compare_fusion
  38.1 1.0 fusion.14
  39.2 0.3 fusion.3
  39.5 0.2 fusion.9
  39.8 0.0 copy-start.7
  39.8 0.5 fusion.1
  40.3 0.7 reshape.134.mixed_ref
  41.1 0.6 reshape.135.gain_ref
  41.7 64.2 %finish.1 = f32[16,2560]{1,0:T(8,128)} custom-call(bf16[16,2560]{1,0:T(8,128)(2,1)} %reshape.134.mixed_ref, bf16[16,2560]{1,0:T(8,128)(2,1)} %copy-done.2, bf16[1,2560]{1,0:T(2,128)(2,1)} %reshape.135.gain_ref, bf16[2560,640]{1,0:T(8,128)(2,1)} %w_out.1, bf16[2560,1792]{1,0:T(8,128)(2,1)} %w_gate.1, bf16[2560,1792]{1,0:T(8,128)(2,1)} %w_up.1, ...), custom_call_target="tpu_custom_call" | custom-call | tf_op jit(solution)/shard_map/finish/pallas_call | solution.py:339
  105.9 1.6 %reshape.136 = f32[4,4,2560]{2,1,0:T(4,128)} reshape(f32[16,2560]{1,0:T(8,128)} %finish.1) | data formatting | bytes 327680 | tf_op jit(solution)/shard_map/reshape | solution.py:475
  (26 shorter events, 0.3 us)
Async XLA Ops:
  0.6 37.5 %copy-start = (bf16[4,4,384,128]{3,2,1,0:T(8,128)(2,1)S(1)}, bf16[4,4,384,128]{3,2,1,0:T(8,128)(2,1)}, u32[]{:S(2)}) copy-start(bf16[4,4,384,128]{3,2,1,0:T(8,128)(2,1)} %param.15) | copy-start | bytes 4718596
  1.7 35.0 %copy-start.2 = (bf16[16,2560]{1,0:T(8,128)(2,1)}, bf16[16,2560]{1,0:T(8,128)(2,1)S(1)}, u32[]{:S(2)}) copy-start(bf16[16,2560]{1,0:T(8,128)(2,1)S(1)} %reshape.128.tokens_ref) | copy-start | bytes 245764
  2.4 1.9 %copy-start.1 = (bf16[2560,640]{1,0:T(8,128)(2,1)S(1)}, bf16[2560,640]{1,0:T(8,128)(2,1)}, u32[]{:S(2)}) copy-start(bf16[2560,640]{1,0:T(8,128)(2,1)} %w_query.1) | copy-start | bytes 9830404
  4.3 1.1 %copy-start.3 = (bf16[2560,128]{1,0:T(8,128)(2,1)S(1)}, bf16[2560,128]{1,0:T(8,128)(2,1)}, u32[]{:S(2)}) copy-start(bf16[2560,128]{1,0:T(8,128)(2,1)} %w_key.1) | copy-start | bytes 1966084
  5.4 1.1 %copy-start.4 = (bf16[2560,128]{1,0:T(8,128)(2,1)S(1)}, bf16[2560,128]{1,0:T(8,128)(2,1)}, u32[]{:S(2)}) copy-start(bf16[2560,128]{1,0:T(8,128)(2,1)} %w_value.1) | copy-start | bytes 1966084
  6.5 30.3 %copy-start.8 = (s32[4]{0:T(128)S(1)}, s32[4]{0:T(128)}, u32[]{:S(2)}) copy-start(s32[4]{0:T(128)} %param.14) | copy-start | bytes 52
  37.2 1.9 %copy-start.6 = (bf16[4,4,4,128]{3,2,1,0:T(4,128)(2,1)}, bf16[4,4,4,128]{3,2,1,0:T(4,128)(2,1)S(1)}, u32[]{:S(2)}) copy-start(bf16[4,4,4,128]{3,2,1,0:T(4,128)(2,1)S(1)} %get-tuple-element.16) | copy-start | bytes 49156
  37.3 2.2 %copy-start.5 = (bf16[4,4,4,128]{3,2,1,0:T(4,128)(2,1)}, bf16[4,4,4,128]{3,2,1,0:T(4,128)(2,1)S(1)}, u32[]{:S(2)}) copy-start(bf16[4,4,4,128]{3,2,1,0:T(4,128)(2,1)S(1)} %get-tuple-element.15) | copy-start | bytes 49156
  38.1 1.6 %copy-start.9 = (bf16[4,4,384,128]{3,2,1,0:T(8,128)(2,1)S(1)}, bf16[4,4,384,128]{3,2,1,0:T(8,128)(2,1)}, u32[]{:S(2)}) copy-start(bf16[4,4,384,128]{3,2,1,0:T(8,128)(2,1)} %param.16) | copy-start | bytes 4718596
  39.8 1.3 %copy-start.7 = (bf16[2560]{0:T(1024)(128)(2,1)S(1)}, bf16[2560]{0:T(1024)(128)(2,1)}, u32[]{:S(2)}) copy-start(bf16[2560]{0:T(1024)(128)(2,1)} %param.18) | copy-start | bytes 15364

commit v2 on v1

--- a/solution.py
+++ b/solution.py
@@ -82,30 +82,39 @@
     right = ring_device((place + 1) % 8)
     left = ring_device((place + 7) % 8)
     half = blocks.shape[2] // 2
-    ups, downs = [], []
+    ups, downs = {}, {}
     for hop in range(4):
         up_owner = ring_device((place + 8 - hop) % 8)
         down_owner = ring_device((place + hop) % 8)
-        up_block, down_block = blocks.at[up_owner], blocks.at[down_owner]
-        if hop == 3:
-            up_block = blocks.at[up_owner, :, pl.ds(0, half)]
-            down_block = blocks.at[down_owner, :, pl.ds(half, half)]
-        if hop > 0:
-            ups[-1].wait_recv()
-        ups.append(
-            send(up_block, up_block, send_sems.at[hop], recv_sems.at[hop], right, narrow)
-        )
-        ups[-1].start()
-        if hop > 0:
-            downs[-1].wait_recv()
-        downs.append(
-            send(down_block, down_block, send_sems.at[4 + hop], recv_sems.at[4 + hop], left, narrow)
-        )
-        downs[-1].start()
-    ups[-1].wait_recv()
-    downs[-1].wait_recv()
-    for copy in ups + downs:
+        for part in range(2):
+            columns = pl.ds(part * half, half)
+            at = hop * 2 + part
+            if hop < 3 or part == 0:
+                block = blocks.at[up_owner, :, columns]
+                if hop > 0:
+                    ups[hop - 1, part].wait_recv()
+                ups[hop, part] = send(
+                    block, block, send_sems.at[at], recv_sems.at[at], right, narrow
+                )
+                ups[hop, part].start()
+            if hop < 3 or part == 1:
+                block = blocks.at[down_owner, :, columns]
+                if hop > 0:
+                    downs[hop - 1, part].wait_recv()
+                downs[hop, part] = send(
+                    block, block, send_sems.at[8 + at], recv_sems.at[8 + at], left, narrow
+                )
+                downs[hop, part].start()
+    for copy in (ups[2, 1], downs[2, 0], ups[3, 0], downs[3, 1]):
+        copy.wait_recv()
+    for copy in list(ups.values()) + list(downs.values()):
         copy.wait_send()
+
+
+def fill_rows(rows, steps_ref):
+    count = steps_ref.shape[1]
+    for step in range(steps_ref.shape[0]):
+        rows[pl.ds(step * count, count), :] = steps_ref[step].astype(jnp.float32)
 
 
 def norm_own(tokens, gain_ref, sums_out, sums_in, send_sem, recv_sem, full_width):
@@ -117,7 +126,9 @@
     copy.wait()
     row_sums = own_sums + sums_in[:, 0:1]
     factor = lax.rsqrt(row_sums / full_width + norm_eps)
-    return (tokens * factor * gain_ref[...].astype(jnp.float32)).astype(jnp.bfloat16)
+    return (tokens * factor * gain_ref[...].astype(jnp.float32).reshape(1, -1)).astype(
+        jnp.bfloat16
+    )
 
 
 def send_to_owners(parts, arrived, send_sems, recv_sems):
@@ -164,7 +175,7 @@
 
 def project_kernel(
     tokens_ref, gain_ref, w_query, w_key, w_value, own_ref,
-    weights, blocks, parts, arrived, sums_out, sums_in,
+    weights, token_rows, blocks, parts, arrived, sums_out, sums_in,
     load_sems, ring_send, ring_recv, part_send, part_recv, sums_send, sums_recv,
 ):
     query_cols, key_cols = w_query.shape[1], w_key.shape[1]
@@ -176,10 +187,10 @@
     for load in loads:
         load.start()
     greet_group()
-    half_width = tokens_ref.shape[1]
-    tokens = tokens_ref[...].astype(jnp.float32)
+    half_width = tokens_ref.shape[2]
+    fill_rows(token_rows, tokens_ref)
     normed = norm_own(
-        tokens, gain_ref, sums_out, sums_in, sums_send.at[0], sums_recv.at[0], 2 * half_width
+        token_rows[...], gain_ref, sums_out, sums_in, sums_send.at[0], sums_recv.at[0], 2 * half_width
     )
     blocks[lax.axis_index("wide")] = normed
     ring_gather(blocks, ring_send, ring_recv)
@@ -187,22 +198,25 @@
         load.wait()
     rows = blocks[...].reshape(-1, half_width)
     sums = jnp.dot(rows, weights[...], preferred_element_type=jnp.float32)
-    parts[...] = sums.reshape(parts.shape)
+    parts[...] = sums.astype(jnp.bfloat16).reshape(parts.shape)
     send_to_owners(parts, arrived, part_send, part_recv)
     for peer in range(4):
-        own_ref[peer] = arrived[2 * peer] + arrived[2 * peer + 1]
+        own_ref[peer] = arrived[2 * peer].astype(jnp.float32) + arrived[2 * peer + 1].astype(
+            jnp.float32
+        )
 
 
 def finish_kernel(
     mixed_ref, tokens_ref, gain_ref, w_out, w_gate, w_up, w_down, result_ref,
     out_weights, gate_weights, up_weights, down_weights,
     mixed_blocks, out_parts, out_arrived, residual, normed_blocks, sums_out, sums_in,
-    lifted, lifted_out, lifted_in, hidden, down_parts, down_arrived,
+    lifted, lifted_out, lifted_in, hidden, down_parts, side_arrived, pair_sums, row_arrived,
     load_sems, mixed_send, mixed_recv, part_send, part_recv, sums_send, sums_recv,
-    normed_send, normed_recv, lifted_send, lifted_recv, down_send, down_recv,
+    normed_send, normed_recv, lifted_send, lifted_recv, side_send, side_recv,
+    row_send, row_recv,
 ):
     wide, narrow = lax.axis_index("wide"), lax.axis_index("narrow")
-    half_width = tokens_ref.shape[1]
+    half_width = tokens_ref.shape[2]
     loads = [
         pltpu.make_async_copy(matrix, place, load_sems.at[i])
         for i, (matrix, place) in enumerate(
@@ -212,6 +226,7 @@
     for load in loads:
         load.start()
     greet_group()
+    fill_rows(residual, tokens_ref)
     mixed_blocks[wide] = mixed_ref[...]
     ring_gather(mixed_blocks, mixed_send, mixed_recv)
     loads[0].wait()
@@ -226,7 +241,7 @@
     for peer in range(4):
         columns = pl.ds(peer * out_cols, out_cols)
         residual[:, columns] = (
-            tokens_ref[:, columns].astype(jnp.float32)
+            residual[:, columns]
             + out_arrived[2 * peer].astype(jnp.float32)
             + out_arrived[2 * peer + 1].astype(jnp.float32)
         )
@@ -265,35 +280,63 @@
 
     lax.fori_loop(0, chunks, activate, 0)
     loads[3].wait()
+    row, side = wide // 2, wide % 2
     down_chunk = 512
-
-    def lower(i, carry):
-        columns = pl.ds(pl.multiple_of(i * down_chunk, down_chunk), down_chunk)
+    chunk_count = half_width // down_chunk
+    side_copies, row_copies = [], []
+
+    def add_side(i):
+        columns = pl.ds(i * down_chunk, down_chunk)
+        side_copies[i].wait_recv()
+        pair_sums[:, :, columns] = (
+            down_parts[side, :, :, columns].astype(jnp.float32)
+            + side_arrived[:, :, columns].astype(jnp.float32)
+        ).astype(jnp.bfloat16)
+        for step in range(1, 4):
+            at = i * 3 + step - 1
+            other = (row + step) % 4
+            row_copies.append(
+                send(
+                    pair_sums.at[other, :, columns],
+                    row_arrived.at[step - 1, :, columns],
+                    row_send.at[at],
+                    row_recv.at[at],
+                    2 * other + side,
+                    narrow,
+                )
+            )
+            row_copies[-1].start()
+
+    for i in range(chunk_count):
+        columns = pl.ds(i * down_chunk, down_chunk)
         sums = jnp.dot(hidden[...], down_weights[:, columns], preferred_element_type=jnp.float32)
-        down_parts[:, :, columns] = sums.astype(jnp.bfloat16).reshape(8, -1, down_chunk)
-        return carry
-
-    lax.fori_loop(0, half_width // down_chunk, lower, 0)
-    copies = []
-    for step in range(1, 8):
-        owner = (wide + step) % 8
-        copies.append(
+        sums = sums.astype(jnp.bfloat16).reshape(4, 2, -1, down_chunk)
+        down_parts[0, :, :, columns] = sums[:, 0]
+        down_parts[1, :, :, columns] = sums[:, 1]
+        side_copies.append(
             send(
-                down_parts.at[owner],
-                down_arrived.at[step - 1],
-                down_send.at[step - 1],
-                down_recv.at[step - 1],
-                owner,
+                down_parts.at[1 - side, :, :, columns],
+                side_arrived.at[:, :, columns],
+                side_send.at[i],
+                side_recv.at[i],
+                2 * row + 1 - side,
                 narrow,
             )
         )
-        copies[-1].start()
-    total = residual[...] + down_parts[wide].astype(jnp.float32)
-    for step, copy in enumerate(copies):
-        copy.wait_recv()
-        total = total + down_arrived[step].astype(jnp.float32)
-    result_ref[...] = total
-    for copy in copies:
+        side_copies[-1].start()
+        if i > 0:
+            add_side(i - 1)
+    add_side(chunk_count - 1)
+    count = result_ref.shape[1]
+    for i in range(chunk_count):
+        columns = pl.ds(i * down_chunk, down_chunk)
+        total = residual[:, columns] + pair_sums[row, :, columns].astype(jnp.float32)
+        for step in range(3):
+            row_copies[i * 3 + step].wait_recv()
+            total = total + row_arrived[step, :, columns].astype(jnp.float32)
+        for step in range(result_ref.shape[0]):
+            result_ref[step, :, columns] = total[step * count : (step + 1) * count]
+    for copy in side_copies + row_copies:
         copy.wait_send()
 
 
@@ -306,7 +349,7 @@
 
 
 def project(tokens, gain, w_query, w_key, w_value):
-    count, half_width = tokens.shape
+    count, half_width = tokens.shape[0] * tokens.shape[1], tokens.shape[2]
     columns = w_query.shape[1] + 2 * w_key.shape[1]
     dma = pltpu.SemaphoreType.DMA
     return pl.pallas_call(
@@ -316,29 +359,30 @@
         out_specs=in_vmem(),
         scratch_shapes=[
             pltpu.VMEM((half_width, columns), jnp.bfloat16),
+            pltpu.VMEM((count, half_width), jnp.float32),
             pltpu.VMEM((8, count, half_width), jnp.bfloat16),
-            pltpu.VMEM((8, count, columns), jnp.float32),
-            pltpu.VMEM((8, count, columns), jnp.float32),
+            pltpu.VMEM((8, count, columns), jnp.bfloat16),
+            pltpu.VMEM((8, count, columns), jnp.bfloat16),
             pltpu.VMEM((count, 128), jnp.float32),
             pltpu.VMEM((count, 128), jnp.float32),
-            dma((3,)), dma((8,)), dma((8,)), dma((8,)), dma((8,)), dma((1,)), dma((1,)),
+            dma((3,)), dma((16,)), dma((16,)), dma((8,)), dma((8,)), dma((1,)), dma((1,)),
         ],
         compiler_params=pltpu.CompilerParams(
-            collective_id=0, has_side_effects=True, vmem_limit_bytes=32 * 2**20
+            collective_id=0, has_side_effects=True, vmem_limit_bytes=56 * 2**20
         ),
         name="project",
-    )(tokens, gain.reshape(1, -1), w_query, w_key, w_value)
+    )(tokens, gain, w_query, w_key, w_value)
 
 
 def finish(mixed, tokens, gain, w_out, w_gate, w_up, w_down):
-    count, half_width = tokens.shape
+    count, half_width = tokens.shape[0] * tokens.shape[1], tokens.shape[2]
     out_cols, ffn_cols = w_out.shape[1], w_gate.shape[1]
     chunk = 256
     chunks = ffn_cols // chunk
     dma = pltpu.SemaphoreType.DMA
     return pl.pallas_call(
         finish_kernel,
-        out_shape=jax.ShapeDtypeStruct((count, half_width), jnp.float32),
+        out_shape=jax.ShapeDtypeStruct(tokens.shape, jnp.float32),
         in_specs=[in_vmem()] * 3 + [in_place()] * 4,
         out_specs=in_vmem(),
         scratch_shapes=[
@@ -357,16 +401,20 @@
             pltpu.VMEM((chunks, 2, 8 * count, chunk), jnp.bfloat16),
             pltpu.VMEM((chunks, 2, 8 * count, chunk), jnp.bfloat16),
             pltpu.VMEM((8 * count, ffn_cols), jnp.bfloat16),
-            pltpu.VMEM((8, count, half_width), jnp.bfloat16),
-            pltpu.VMEM((7, count, half_width), jnp.bfloat16),
-            dma((4,)), dma((8,)), dma((8,)), dma((8,)), dma((8,)), dma((1,)), dma((1,)),
-            dma((8,)), dma((8,)), dma((chunks,)), dma((chunks,)), dma((7,)), dma((7,)),
+            pltpu.VMEM((2, 4, count, half_width), jnp.bfloat16),
+            pltpu.VMEM((4, count, half_width), jnp.bfloat16),
+            pltpu.VMEM((4, count, half_width), jnp.bfloat16),
+            pltpu.VMEM((3, count, half_width), jnp.bfloat16),
+            dma((4,)), dma((16,)), dma((16,)), dma((8,)), dma((8,)), dma((1,)), dma((1,)),
+            dma((16,)), dma((16,)), dma((chunks,)), dma((chunks,)),
+            dma((half_width // 512,)), dma((half_width // 512,)),
+            dma((3 * (half_width // 512),)), dma((3 * (half_width // 512),)),
         ],
         compiler_params=pltpu.CompilerParams(
             collective_id=1, has_side_effects=True, vmem_limit_bytes=56 * 2**20
         ),
         name="finish",
-    )(mixed, tokens, gain.reshape(1, -1), w_out, w_gate, w_up, w_down)
+    )(mixed, tokens, gain, w_out, w_gate, w_up, w_down)
 
 
 def shards(
@@ -402,7 +450,7 @@
         lax.axis_size("wide") == 8 and query_cols % 128 == 0 and ffn_cols % 256 == 0
     )
     if by_kernel:
-        own = project(own_rows, gain_attn, w_query, w_key, w_value)
+        own = project(embeds, gain_attn, w_query, w_key, w_value)
         own = jnp.transpose(own, (1, 0, 2))
     else:
         attn_sums = lax.psum(jnp.sum(tokens * tokens, axis=1), "narrow")
@@ -471,8 +519,8 @@
         STEPS * local_rolls, heads_local * HD
     )
     if by_kernel:
-        result = finish(mixed_heads, own_rows, gain_ffn, w_out, w_gate, w_up, w_down)
-        return (result.reshape(STEPS, local_rolls, half_width), keys_now, values_now)
+        result = finish(mixed_heads, embeds, gain_ffn, w_out, w_gate, w_up, w_down)
+        return (result, keys_now, values_now)
     out_part = jnp.dot(
         lax.all_gather(mixed_heads, "wide", axis=0, tiled=True),
         w_out,

time: 108 us -> 101 us (0.935)
  the two profiles are of different devices: /device:TPU:13 before, /device:TPU:0 now
where the time goes in v2:
time: 101 us
  Pallas kernels  92.2 us (91%)
  local copies, waits for them, and re-layouts  3.78 us (4%)
  other arithmetic  2.41 us (2%)
  matrix products  1.9 us (2%)
    pallas_call x1, Pallas kernels, finish(): pl.pallas_call(finish_kernel, out_shape=jax.ShapeDtypeStruct(tokens.shape...  63.9 us
    pallas_call x1, Pallas kernels, project(): pl.pallas_call(project_kernel, out_shape=jax.ShapeDtypeStruct((4, count,...  28.3 us

profile of v2, /device:TPU:0, one launch (start us, length us, event | category | flops | bytes accessed | tf_op | source)
XLA Modules:
  0.0 101.2 jit_solution(3756212865822075119)
XLA Ops:
  0.6 0.0 copy-start
  0.7 0.8 iota_compare_fusion
  1.5 0.7 add_convert_fusion.2
  2.3 0.1 multiply_cosine_fusion
  2.4 28.3 %project.1 = f32[4,16,896]{2,1,0:T(8,128)} custom-call(bf16[4,4,2560]{2,1,0:T(4,128)(2,1)} %tokens_ref.3, bf16[2560]{0:T(1024)(128)(2,1)} %gain_ref.2, bf16[2560,640]{1,0:T(8,128)(2,1)} %w_query.1, bf16[2560,128]{1,0:T(8,128)(2,1)} %w_key.1, bf16[2560,128]{1,0:T(8,128)(2,1)} %w_value.1), custom_call_target="tpu_custom_call" | custom-call | tf_op jit(solution)/shard_map/project/pallas_call | solution.py:355
  30.8 1.0 reshape.116
  31.8 0.1 fusion.13
  31.9 0.1 copy.35
  32.0 0.1 fusion.10
  32.1 0.0 copy-start.2
  32.1 0.0 copy-start.1
  32.1 0.1 reshape.117
  32.2 0.1 subtract_convert_fusion
  32.4 0.1 maximum_bitcast_fusion
  32.6 0.2 fusion.15
  32.8 0.0 copy-done
  32.8 0.0 copy-start.3
  32.8 1.0 %fusion.14 = (f32[4,4,20]{2,1,0:T(4,128)S(1)}, f32[4,4,20,384]{3,2,1,0:T(8,128)S(1)}) fusion(bf16[4,4,384,128]{3,2,1,0:T(8,128)(2,1)S(1)} %copy-done, bf16[4,4,20,128]{3,1,2,0:T(4,128)(2,1)S(1)} %bitcast.21, pred[4,384]{1,0:T(4,128)(4,1)S(1)} %iota_compare_fusion), kind=kOutput, calls=%fused_computation.38 | convolution fusion | flops 31825600 | bytes 2149120 | tf_op jit(solution)/shard_map/rkqd,rkcd->rkqc/dot_general | solution.py:485
  33.8 0.0 copy-done.2
  33.9 0.3 fusion.3
  34.1 0.0 copy-done.1
  34.1 0.2 fusion.9
  34.4 0.0 copy-done.3
  34.4 0.5 fusion.1
  34.9 0.7 reshape.120.mixed_ref
  35.7 63.9 %finish.1 = f32[4,4,2560]{2,1,0:T(4,128)} custom-call(bf16[16,2560]{1,0:T(8,128)(2,1)} %reshape.120.mixed_ref, bf16[4,4,2560]{2,1,0:T(4,128)(2,1)} %tokens_ref.3, bf16[2560]{0:T(1024)(128)(2,1)} %gain_ref.3, bf16[2560,640]{1,0:T(8,128)(2,1)} %w_out.1, bf16[2560,1792]{1,0:T(8,128)(2,1)} %w_gate.1, bf16[2560,1792]{1,0:T(8,128)(2,1)} %w_up.1, ...), custom_call_target="tpu_custom_call" | custom-call | tf_op jit(solution)/shard_map/finish/pallas_call | solution.py:383
  99.6 1.6 %copy.55 = f32[4,4,2560]{2,1,0:T(4,128)} copy(f32[4,4,2560]{2,1,0:T(4,128)} %finish.1) | data formatting | bytes 327680
  (16 shorter events, 0.3 us)
Async XLA Ops:
  0.6 32.1 %copy-start = (bf16[4,4,384,128]{3,2,1,0:T(8,128)(2,1)S(1)}, bf16[4,4,384,128]{3,2,1,0:T(8,128)(2,1)}, u32[]{:S(2)}) copy-start(bf16[4,4,384,128]{3,2,1,0:T(8,128)(2,1)} %param.15) | copy-start | bytes 4718596
  32.1 1.7 %copy-start.2 = (bf16[4,4,4,128]{3,2,1,0:T(4,128)(2,1)}, bf16[4,4,4,128]{3,2,1,0:T(4,128)(2,1)S(1)}, u32[]{:S(2)}) copy-start(bf16[4,4,4,128]{3,2,1,0:T(4,128)(2,1)S(1)} %get-tuple-element.21) | copy-start | bytes 49156
  32.1 2.0 %copy-start.1 = (bf16[4,4,4,128]{3,2,1,0:T(4,128)(2,1)}, bf16[4,4,4,128]{3,2,1,0:T(4,128)(2,1)S(1)}, u32[]{:S(2)}) copy-start(bf16[4,4,4,128]{3,2,1,0:T(4,128)(2,1)S(1)} %get-tuple-element.22) | copy-start | bytes 49156
  32.8 1.6 %copy-start.3 = (bf16[4,4,384,128]{3,2,1,0:T(8,128)(2,1)S(1)}, bf16[4,4,384,128]{3,2,1,0:T(8,128)(2,1)}, u32[]{:S(2)}) copy-start(bf16[4,4,384,128]{3,2,1,0:T(8,128)(2,1)} %param.16) | copy-start | bytes 4718596

commit v3 on v2

--- a/solution.py
+++ b/solution.py
@@ -37,16 +37,6 @@
 def scale_rows(tokens, row_sums, gain_row, full_width):
     factor = lax.rsqrt(row_sums / full_width + norm_eps)
     return (tokens * factor[:, None] * gain_row.astype(jnp.float32)).astype(jnp.bfloat16)
-
-
-def ring_place(device):
-    row, side = device // 2, device % 2
-    return row + side * (7 - 2 * row)
-
-
-def ring_device(place):
-    side = place // 4
-    return 2 * (place + side * (7 - 2 * place)) + side
 
 
 def greet_group():
@@ -76,38 +66,32 @@
     )
 
 
-def ring_gather(blocks, send_sems, recv_sems):
+def gather_blocks(blocks, send_sems, recv_sems):
     wide, narrow = lax.axis_index("wide"), lax.axis_index("narrow")
-    place = ring_place(wide)
-    right = ring_device((place + 1) % 8)
-    left = ring_device((place + 7) % 8)
+    row, side = wide // 2, wide % 2
+    beside = 2 * row + 1 - side
     half = blocks.shape[2] // 2
-    ups, downs = {}, {}
-    for hop in range(4):
-        up_owner = ring_device((place + 8 - hop) % 8)
-        down_owner = ring_device((place + hop) % 8)
-        for part in range(2):
-            columns = pl.ds(part * half, half)
-            at = hop * 2 + part
-            if hop < 3 or part == 0:
-                block = blocks.at[up_owner, :, columns]
-                if hop > 0:
-                    ups[hop - 1, part].wait_recv()
-                ups[hop, part] = send(
-                    block, block, send_sems.at[at], recv_sems.at[at], right, narrow
-                )
-                ups[hop, part].start()
-            if hop < 3 or part == 1:
-                block = blocks.at[down_owner, :, columns]
-                if hop > 0:
-                    downs[hop - 1, part].wait_recv()
-                downs[hop, part] = send(
-                    block, block, send_sems.at[8 + at], recv_sems.at[8 + at], left, narrow
-                )
-                downs[hop, part].start()
-    for copy in (ups[2, 1], downs[2, 0], ups[3, 0], downs[3, 1]):
+
+    def share(owner, part, at, target):
+        block = blocks.at[owner, :, pl.ds(part * half, half)]
+        at = part * 8 + at
+        return send(block, block, send_sems.at[at], recv_sems.at[at], target, narrow)
+
+    along, across = {}, []
+    for part in range(2):
+        for step in range(1, 4):
+            along[part, step] = share(wide, part, step, 2 * ((row + step) % 4) + side)
+            along[part, step].start()
+        across.append(share(wide, part, 0, beside))
+        across[-1].start()
+    for part in range(2):
+        for step in range(1, 4):
+            along[part, step].wait_recv()
+            across.append(share(2 * ((row + 4 - step) % 4) + side, part, 3 + step, beside))
+            across[-1].start()
+    for copy in across:
         copy.wait_recv()
-    for copy in list(ups.values()) + list(downs.values()):
+    for copy in list(along.values()) + across:
         copy.wait_send()
 
 
@@ -193,7 +177,7 @@
         token_rows[...], gain_ref, sums_out, sums_in, sums_send.at[0], sums_recv.at[0], 2 * half_width
     )
     blocks[lax.axis_index("wide")] = normed
-    ring_gather(blocks, ring_send, ring_recv)
+    gather_blocks(blocks, ring_send, ring_recv)
     for load in loads:
         load.wait()
     rows = blocks[...].reshape(-1, half_width)
@@ -228,7 +212,7 @@
     greet_group()
     fill_rows(residual, tokens_ref)
     mixed_blocks[wide] = mixed_ref[...]
-    ring_gather(mixed_blocks, mixed_send, mixed_recv)
+    gather_blocks(mixed_blocks, mixed_send, mixed_recv)
     loads[0].wait()
     out_sums = jnp.dot(
         mixed_blocks[...].reshape(-1, half_width),
@@ -248,7 +232,7 @@
     normed_blocks[wide] = norm_own(
         residual[...], gain_ref, sums_out, sums_in, sums_send.at[0], sums_recv.at[0], 2 * half_width
     )
-    ring_gather(normed_blocks, normed_send, normed_recv)
+    gather_blocks(normed_blocks, normed_send, normed_recv)
     loads[1].wait()
     loads[2].wait()
     chunks, chunk = lifted.shape[0], lifted.shape[3]

time: 101 us -> 95 us (0.941)
  Pallas kernels: 92.2 us -> 85.8 us
    pallas_call x1, Pallas kernels: 63.9 us -> 60.5 us  [finish(): pl.pallas_call(finish_kernel, out_shape=jax.ShapeDtypeStruct(tokens.shape...]
    pallas_call x1, Pallas kernels: 28.3 us -> 25.3 us  [project(): pl.pallas_call(project_kernel, out_shape=jax.ShapeDtypeStruct((4, count,...]
where the time goes in v3:
time: 95 us; the launch traced here: 94.7 us
  Pallas kernels  85.8 us (90%)
  local copies, waits for them, and re-layouts  3.78 us (4%)
  other arithmetic  2.41 us (3%)
  matrix products  1.9 us (2%)
    pallas_call x1, Pallas kernels, finish(): pl.pallas_call(finish_kernel, out_shape=jax.ShapeDtypeStruct(tokens.shape...  60.5 us
    pallas_call x1, Pallas kernels, project(): pl.pallas_call(project_kernel, out_shape=jax.ShapeDtypeStruct((4, count,...  25.3 us

profile of v3, /device:TPU:0, one launch (start us, length us, event | category | flops | bytes accessed | tf_op | source)
XLA Modules:
  0.0 94.7 jit_solution(8339546668082259287)
XLA Ops:
  0.6 0.0 copy-start
  0.7 0.8 iota_compare_fusion
  1.5 0.7 add_convert_fusion.2
  2.3 0.1 multiply_cosine_fusion
  2.4 25.3 %project.1 = f32[4,16,896]{2,1,0:T(8,128)} custom-call(bf16[4,4,2560]{2,1,0:T(4,128)(2,1)} %tokens_ref.3, bf16[2560]{0:T(1024)(128)(2,1)} %gain_ref.2, bf16[2560,640]{1,0:T(8,128)(2,1)} %w_query.1, bf16[2560,128]{1,0:T(8,128)(2,1)} %w_key.1, bf16[2560,128]{1,0:T(8,128)(2,1)} %w_value.1), custom_call_target="tpu_custom_call" | custom-call | tf_op jit(solution)/shard_map/project/pallas_call | solution.py:339
  27.7 1.0 %reshape.116 = f32[4,4,4,896]{3,1,0,2:T(4,128)S(1)} reshape(f32[16,4,896]{2,0,1:T(8,128)} %bitcast.19) | data formatting | bytes 458752 | tf_op jit(solution)/shard_map/reshape | solution.py:453
  28.8 0.1 fusion.13
  28.9 0.1 copy.35
  29.0 0.1 fusion.10
  29.1 0.0 copy-start.2
  29.1 0.0 copy-start.1
  29.1 0.1 reshape.117
  29.2 0.1 subtract_convert_fusion
  29.4 0.1 maximum_bitcast_fusion
  29.6 0.2 fusion.15
  29.7 0.0 copy-done
  29.8 0.0 copy-start.3
  29.8 1.0 %fusion.14 = (f32[4,4,20]{2,1,0:T(4,128)S(1)}, f32[4,4,20,384]{3,2,1,0:T(8,128)S(1)}) fusion(bf16[4,4,384,128]{3,2,1,0:T(8,128)(2,1)S(1)} %copy-done, bf16[4,4,20,128]{3,1,2,0:T(4,128)(2,1)S(1)} %bitcast.21, pred[4,384]{1,0:T(4,128)(4,1)S(1)} %iota_compare_fusion), kind=kOutput, calls=%fused_computation.38 | convolution fusion | flops 31825600 | bytes 2149120 | tf_op jit(solution)/shard_map/rkqd,rkcd->rkqc/dot_general | solution.py:469
  30.8 0.0 copy-done.2
  30.8 0.3 fusion.3
  31.1 0.0 copy-done.1
  31.1 0.2 fusion.9
  31.4 0.0 copy-done.3
  31.4 0.5 fusion.1
  31.9 0.7 reshape.120.mixed_ref
  32.7 60.5 %finish.1 = f32[4,4,2560]{2,1,0:T(4,128)} custom-call(bf16[16,2560]{1,0:T(8,128)(2,1)} %reshape.120.mixed_ref, bf16[4,4,2560]{2,1,0:T(4,128)(2,1)} %tokens_ref.3, bf16[2560]{0:T(1024)(128)(2,1)} %gain_ref.3, bf16[2560,640]{1,0:T(8,128)(2,1)} %w_out.1, bf16[2560,1792]{1,0:T(8,128)(2,1)} %w_gate.1, bf16[2560,1792]{1,0:T(8,128)(2,1)} %w_up.1, ...), custom_call_target="tpu_custom_call" | custom-call | tf_op jit(solution)/shard_map/finish/pallas_call | solution.py:367
  93.1 1.6 %copy.55 = f32[4,4,2560]{2,1,0:T(4,128)} copy(f32[4,4,2560]{2,1,0:T(4,128)} %finish.1) | data formatting | bytes 327680
  (16 shorter events, 0.3 us)
Async XLA Ops:
  0.6 29.1 %copy-start = (bf16[4,4,384,128]{3,2,1,0:T(8,128)(2,1)S(1)}, bf16[4,4,384,128]{3,2,1,0:T(8,128)(2,1)}, u32[]{:S(2)}) copy-start(bf16[4,4,384,128]{3,2,1,0:T(8,128)(2,1)} %param.15) | copy-start | bytes 4718596
  29.1 1.7 %copy-start.2 = (bf16[4,4,4,128]{3,2,1,0:T(4,128)(2,1)}, bf16[4,4,4,128]{3,2,1,0:T(4,128)(2,1)S(1)}, u32[]{:S(2)}) copy-start(bf16[4,4,4,128]{3,2,1,0:T(4,128)(2,1)S(1)} %get-tuple-element.21) | copy-start | bytes 49156
  29.1 2.0 %copy-start.1 = (bf16[4,4,4,128]{3,2,1,0:T(4,128)(2,1)}, bf16[4,4,4,128]{3,2,1,0:T(4,128)(2,1)S(1)}, u32[]{:S(2)}) copy-start(bf16[4,4,4,128]{3,2,1,0:T(4,128)(2,1)S(1)} %get-tuple-element.22) | copy-start | bytes 49156
  29.8 1.6 %copy-start.3 = (bf16[4,4,384,128]{3,2,1,0:T(8,128)(2,1)S(1)}, bf16[4,4,384,128]{3,2,1,0:T(8,128)(2,1)}, u32[]{:S(2)}) copy-start(bf16[4,4,384,128]{3,2,1,0:T(8,128)(2,1)} %param.16) | copy-start | bytes 4718596
